TPU v7x, 32 devices: a whole 2x2x4 slice. The times are simulated.
32 devices in a mesh: dp: 8 (over z, core), tensor: 4 (over y, x).
Axes of the slice: x: 2, y: 2, z: 4, core: 2. Of those that a mesh axis runs over, the one named last changes fastest.
Arguments:
- x_rows: bfloat16 [256, 12288], P(('dp', 'tensor')), may hold values from -6 to 6
- block_weights: bfloat16 [1568, 128, 128], P(('dp', 'tensor')), may hold values from -0.25 to 0.25
- block_row: int32 [1568], P(('dp', 'tensor')), may hold values from 0 to 95, as said below
- block_col: int32 [1568], P(('dp', 'tensor')), may hold values from 0 to 383, as said below
- block_counts: int32 [32], P(('dp', 'tensor')), may hold values from 0 to 49, as said below
- act_grad: bfloat16 [256, 49152], P('dp', 'tensor'), may hold values from -0.75 to 0.75
Outputs:
- activation: bfloat16 [256, 49152], P('dp', 'tensor')
- grad_blocks: bfloat16 [1568, 128, 128], P(('dp', 'tensor'))
Inputs may be any that keep to these rules, and one draw needn't show every extreme that they name: `block_row`: live slots of the devices with tensor index t hold, without repeats, the blocks of a butterfly pattern over the column blocks t * 96 to (t + 1) * 96 - 1: there are 96 distinct row blocks r_0 to r_(95) for t, and column block t * 96 + j has the 4 row blocks r_(j XOR o) for o in 0, 1, 2, 4. Slots that are not live hold arbitrary indices in range. `block_col`: A live slot of a device with tensor index t names a column block of t * 96 to (t + 1) * 96 - 1, and so does every other slot of that device. `block_counts`: the counts of the devices with one tensor index sum to 384; some device has 49.
All inputs are finite; a program needn't handle non-finite values.
Results may differ from a plain program's by a relative error of at most 0.014.
Values may be sent and summed in bfloat16 or wider, within the bound.
A program may use at most 64 MiB of HBM per device.

v0:
```python
import math

import jax
import jax.numpy as jnp
from jax import lax
from jax.sharding import PartitionSpec as P


def gelu_tanh(value):
    return jax.nn.gelu(value, approximate=True)


def per_device(x_rows, block_weights, block_row, block_col, block_counts, act_grad):
    rank = lax.axis_index("tensor")
    n_data = lax.axis_size("dp")
    cap, edge = (block_weights.shape[0], block_weights.shape[1])
    tok_rows, width = x_rows.shape
    row_blocks = width // edge
    rows, local_width = act_grad.shape
    col_blocks = local_width // edge
    slot_ids = jnp.arange(cap, dtype=jnp.int32)
    alive = slot_ids < block_counts[0]
    col_local = jnp.where(alive, block_col - rank * col_blocks, -1)
    gathered = lax.all_gather(x_rows, "tensor", axis=0, tiled=True)
    features = gathered.reshape(rows, row_blocks, edge)
    total_slots = n_data * cap
    start = jnp.int32(0)
    pre_three = jnp.zeros((rows, col_blocks, edge), jnp.float32)
    accumulate_all_index = jnp.zeros((total_slots,), jnp.int32)
    accumulate_all_col = jnp.zeros((total_slots,), jnp.int32)
    weights = lax.all_gather(block_weights, "dp", axis=0, tiled=True)
    indices = lax.all_gather(block_row, "dp", axis=0, tiled=True)
    targets = lax.all_gather(col_local, "dp", axis=0, tiled=True)
    count = weights.shape[0]
    group = math.gcd(count, 16)

    def one_group(acc, item):
        w_group, i_group, c_group = item
        selected = jnp.take(features, i_group, axis=1)
        product = jnp.einsum("rgk,gkm->rgm", selected, w_group, preferred_element_type=jnp.float32)
        for member in range(group):
            target = c_group[member]
            switch = (target >= 0).astype(jnp.float32)
            place = jnp.clip(target, 0, col_blocks - 1)
            current = lax.dynamic_index_in_dim(acc, place, 1, keepdims=False)
            acc = lax.dynamic_update_index_in_dim(
                acc, current + product[:, member, :] * switch, place, 1
            )
        return (acc, None)

    items = (
        weights.reshape(count // group, group, edge, edge),
        indices.reshape(count // group, group),
        targets.reshape(count // group, group),
    )
    pre_three, _ = lax.scan(one_group, pre_three, items)
    accumulate_all_index = lax.dynamic_update_slice_in_dim(accumulate_all_index, indices, start, 0)
    accumulate_all_col = lax.dynamic_update_slice_in_dim(accumulate_all_col, targets, start, 0)
    pre_three, all_index, all_col = (pre_three, accumulate_all_index, accumulate_all_col)
    pre = pre_three.reshape(rows, local_width)
    act, back = jax.vjp(gelu_tanh, pre)
    activation = act.astype(jnp.bfloat16)
    (pre_grad,) = back(act_grad.astype(jnp.float32))
    grad_three = pre_grad.astype(jnp.bfloat16).reshape(rows, col_blocks, edge)
    indices = all_index
    targets = all_col
    selected = jnp.take(features, indices, axis=1)
    switch = (targets >= 0).astype(jnp.bfloat16)
    chosen = (
        jnp.take(grad_three, jnp.clip(targets, 0, col_blocks - 1), axis=1) * switch[None, :, None]
    )
    grads = lax.psum_scatter(
        jnp.einsum("rnk,rnm->nkm", selected, chosen, preferred_element_type=jnp.float32).astype(
            jnp.bfloat16
        ),
        "dp",
        scatter_dimension=0,
        tiled=True,
    )
    return (activation, grads)


def solution(mesh):
    return jax.shard_map(
        per_device,
        mesh=mesh,
        in_specs=(
            P(("dp", "tensor"), None),
            P(("dp", "tensor"), None, None),
            P(("dp", "tensor")),
            P(("dp", "tensor")),
            P(("dp", "tensor")),
            P("dp", "tensor"),
        ),
        out_specs=(P("dp", "tensor"), P(("dp", "tensor"), None, None)),
        check_vma=False,
    )
```

profile of v0, /device:TPU:0, one launch (start us, length us, event | category | flops | bytes accessed | tf_op | source)
XLA Modules:
  0.0 908.3 jit_solution(10403835807140596671)
XLA Ops:
  10.2 10.6 %all-reduce.2 = (s32[392]{0:T(512)S(1)}, s32[392]{0:T(512)S(1)}) all-reduce(s32[392]{0:T(512)S(1)} %fusion.44, s32[392]{0:T(512)S(1)} %dynamic-update-slice.1), channel_id=1, replica_groups=mesh['dp'=8,'tensor'=4] {'dp'}, use_global_device_ids=true, to_apply=%add | all-reduce | flops 784 | bytes 6272
  21.1 11.7 %all_gather.15 = bf16[32,12288]{1,0:T(8,128)(2,1)S(1)} all-gather(bf16[8,12288]{1,0:T(8,128)(2,1)S(1)} %copy-done.1), channel_id=1, replica_groups=mesh['dp'=8,'tensor'=4] {'tensor'}, dimensions={0}, use_global_device_ids=true | all-gather | bytes 983040 | tf_op jit(solution)/shard_map/all_gather | solution.py:24
  32.9 3.2 gather_fusion.1
  36.2 95.1 %all-gather.2.cloned.1.call-done = bf16[392,128,128]{2,1,0:T(8,128)(2,1)} async-done(((bf16[49,128,128]{2,1,0:T(8,128)(2,1)}), bf16[392,128,128]{2,1,0:T(8,128)(2,1)}) %all-gather.2.cloned.1.call-update) | async-done | bytes 12845072 | tf_op jit(solution)/shard_map/all_gather | solution.py:31
  131.5 623.1 %while.10 = (s32[]{:T(128)}, f32[32,96,128]{2,0,1:T(8,128)S(1)}, s32[49,8]{1,0:T(8,128)S(1)}, bf16[49,8,128,128]{3,2,1,0:T(8,128)(2,1)}, s32[49,8]{1,0:T(8,128)S...) while((s32[]{:T(128)}, f32[32,96,128]{2,0,1:T(8,128)S(1)}, ...), condition=%wide.region_1.2_spmd, body=%wide.region_0.1_spmd.sunk | while | flops 8488042 | bytes 987925 | solution.py:56
  142.9 1.2 convolution_bitcast_fusion.2
  155.6 1.2 convolution_bitcast_fusion.2
  168.3 1.2 convolution_bitcast_fusion.2
  181.0 1.2 convolution_bitcast_fusion.2
  193.7 1.2 convolution_bitcast_fusion.2
  206.5 1.2 convolution_bitcast_fusion.2
  219.2 1.2 convolution_bitcast_fusion.2
  244.6 1.2 convolution_bitcast_fusion.2
  257.3 1.2 convolution_bitcast_fusion.2
  270.0 1.2 convolution_bitcast_fusion.2
  282.7 1.2 convolution_bitcast_fusion.2
  308.2 1.2 convolution_bitcast_fusion.2
  320.9 1.2 convolution_bitcast_fusion.2
  333.6 1.2 convolution_bitcast_fusion.2
  346.3 1.2 convolution_bitcast_fusion.2
  371.8 1.2 convolution_bitcast_fusion.2
  384.5 1.2 convolution_bitcast_fusion.2
  397.2 1.2 convolution_bitcast_fusion.2
  409.9 1.2 convolution_bitcast_fusion.2
  422.6 1.2 convolution_bitcast_fusion.2
  435.3 1.2 convolution_bitcast_fusion.2
  448.1 1.2 convolution_bitcast_fusion.2
  460.8 1.2 convolution_bitcast_fusion.2
  486.2 1.2 convolution_bitcast_fusion.2
  498.9 1.2 convolution_bitcast_fusion.2
  511.6 1.2 convolution_bitcast_fusion.2
  524.4 1.2 convolution_bitcast_fusion.2
  549.8 1.2 convolution_bitcast_fusion.2
  562.5 1.2 convolution_bitcast_fusion.2
  575.2 1.2 convolution_bitcast_fusion.2
  587.9 1.2 convolution_bitcast_fusion.2
  613.4 1.2 convolution_bitcast_fusion.2
  626.1 1.2 convolution_bitcast_fusion.2
  638.8 1.2 convolution_bitcast_fusion.2
  651.5 1.2 convolution_bitcast_fusion.2
  664.2 1.2 convolution_bitcast_fusion.2
  677.0 1.2 convolution_bitcast_fusion.2
  689.7 1.2 convolution_bitcast_fusion.2
  702.4 1.2 convolution_bitcast_fusion.2
  754.6 2.1 fusion.43
  756.8 3.2 gather_fusion.2
  760.0 11.3 %convolution_convert_fusion = bf16[392,128,128]{2,1,0:T(8,128)(2,1)} fusion(bf16[392,32,128]{2,1,0:T(8,128)(2,1)} %gather_fusion.2, bf16[392,32,128]{2,1,0:T(8,128)(2,1)} %gather_fusion.1, pred[392]{0:T(512)(128)(4,1)S(1)} %get-tuple-element.79, pred[392]{0:T(512)(128)(4,1)S(1)} %compare_and_fusion.2, bf16[392]{0:T(512)(128)(2,1)S(1)} %get-tuple-element.78), kind=kOutput, calls=%fused_computation.43 | convolution fusion | flops 422281216 | bytes 19269152 | tf_op jit(solution)/shard_map/rnk,rnm->nkm/dot_general | solution.py:73
  771.3 130.1 %reduce-scatter.2.cloned.1.call-done = bf16[49,128,128]{2,1,0:T(8,128)(2,1)} async-done(((bf16[392,128,128]{2,1,0:T(8,128)(2,1)}), bf16[49,128,128]{2,1,0:T(8,128)(2,1)}) %reduce-scatter.2.cloned.1.call-update) | async-done | bytes 1605648 | tf_op jit(solution)/shard_map/reduce_scatter | solution.py:72
  (726 shorter events, 81.3 us)
Async XLA Ops:
  7.2 1.5 copy-start.4
  7.2 2.7 copy-start.3
  7.2 3.0 copy-start.2
  7.2 13.9 %copy-start.1 = (bf16[8,12288]{1,0:T(8,128)(2,1)S(1)}, bf16[8,12288]{1,0:T(8,128)(2,1)}, u32[]{:S(2)}) copy-start(bf16[8,12288]{1,0:T(8,128)(2,1)} %param.10) | copy-start | bytes 589828
  7.2 124.1 %all-gather.2.cloned.1.call-start = ((), (), s32[]{:S(2)}) async-start(), calls=%async_computation.1 | async-start | bytes 14450688 | tf_op jit(solution)/shard_map/all_gather | solution.py:31
  7.9 893.5 %reduce-scatter.2.cloned.1.call-start = ((), (), s32[]{:S(2)}) async-start(), calls=%async_computation.2 | async-start | bytes 14450688 | tf_op jit(solution)/shard_map/reduce_scatter | solution.py:72
  131.5 623.1 %copy-start = (bf16[32,12288]{1,0:T(8,128)(2,1)S(1)}, bf16[32,12288]{1,0:T(8,128)(2,1)}, u32[]{:S(2)}) copy-start(bf16[32,12288]{1,0:T(8,128)(2,1)} %param.15) | copy-start | bytes 2359300
Sparse Core Ops, SparseCore 0:
  9.7 121.5 all-gather.1
  771.5 129.9 reduce-scatter.1
where the time goes:
time: 917 us; the launch traced here: 908 us
  loops' own time  498 us (54%)
  waiting for transfers between devices  226 us (25%)
  matrix products  69.3 us (8%)
  local copies, waits for them, and re-layouts  68.4 us (7%)
  blocking collectives  22.3 us (2%)
  between operations  15.5 us (2%)
    another operation x1, loops' own time, per_device(): pre_three, _ = lax.scan(one_group, pre_three, items)  498 us
    reduce_scatter x1, waiting for transfers between devices, per_device(): lax.psum_scatter(jnp.einsum('rnk,rnm->nkm', selected, chosen, preferred_e...  130 us
    all_gather x1, waiting for transfers between devices, per_device(): weights = lax.all_gather(block_weights, 'dp', axis=0, tiled=True)  95.1 us
    dot_general x49, matrix products, one_group(): jnp.einsum('rgk,gkm->rgm', selected, w_group, preferred_element_type=jnp....  58.1 us
    slice x49, local copies, waits for them, and re-layouts, one_group(): target = c_group[member]  32.4 us
    gather x49, local copies, waits for them, and re-layouts, one_group(): selected = jnp.take(features, i_group, axis=1)  27.6 us
  transfers between devices with their start and end apart: 2, of which 2 were waited for; matrix products, arithmetic and copies ran while one was open for 0% of the time, Pallas kernels for 0%

commit v1 on v0

--- a/solution.py
+++ b/solution.py
@@ -1,8 +1,11 @@
+import functools
 import math
 
 import jax
 import jax.numpy as jnp
 from jax import lax
+from jax.experimental import pallas as pl
+from jax.experimental.pallas import tpu as pltpu
 from jax.sharding import PartitionSpec as P
 
 
@@ -10,7 +13,92 @@
     return jax.nn.gelu(value, approximate=True)
 
 
-def per_device(x_rows, block_weights, block_row, block_col, block_counts, act_grad):
+def forward_kernel(row_ref, col_ref, count_ref, x_ref, w_ref, out_ref, acc_ref):
+    cap, edge, _ = w_ref.shape
+    blocks = acc_ref.shape[1] // edge
+
+    @pl.loop(0, blocks)
+    def _(block):
+        lanes = pl.ds(pl.multiple_of(block * edge, edge), edge)
+        acc_ref[:, lanes] = jnp.zeros((acc_ref.shape[0], edge), jnp.float32)
+
+    @pl.loop(0, count_ref[0])
+    def _(slot):
+        source = pl.ds(pl.multiple_of(row_ref[slot] * edge, edge), edge)
+        target = pl.ds(pl.multiple_of(col_ref[slot] * edge, edge), edge)
+        acc_ref[:, target] += jnp.dot(
+            x_ref[:, source], w_ref[slot], preferred_element_type=jnp.float32
+        )
+
+    @pl.loop(0, blocks)
+    def _(block):
+        lanes = pl.ds(pl.multiple_of(block * edge, edge), edge)
+        out_ref[:, lanes] = acc_ref[:, lanes].astype(out_ref.dtype)
+
+
+def gradient_kernel(row_ref, col_ref, count_ref, x_ref, grad_ref, out_ref):
+    cap, edge, _ = out_ref.shape
+
+    @pl.loop(0, cap)
+    def _(slot):
+        source = pl.ds(pl.multiple_of(row_ref[slot] * edge, edge), edge)
+        target = pl.ds(pl.multiple_of(col_ref[slot] * edge, edge), edge)
+        product = lax.dot_general(
+            x_ref[:, source],
+            grad_ref[:, target],
+            (((0,), (0,)), ((), ())),
+            preferred_element_type=jnp.float32,
+        )
+        out_ref[slot] = jnp.where(slot < count_ref[0], product, 0.0).astype(out_ref.dtype)
+
+
+SMEM = pl.BlockSpec(memory_space=pltpu.SMEM)
+VMEM = pl.BlockSpec(memory_space=pltpu.VMEM)
+PARAMS = pltpu.CompilerParams(vmem_limit_bytes=48 * 1024 * 1024)
+
+
+def move_rows(x_rows, block_weights, block_row, block_col, block_counts, act_grad):
+    rank = lax.axis_index("tensor")
+    cap, edge = (block_weights.shape[0], block_weights.shape[1])
+    width = x_rows.shape[1]
+    tokens = x_rows.shape[0] * lax.axis_size("dp") * lax.axis_size("tensor")
+    local_width = act_grad.shape[1]
+    col_local = block_col - rank * (local_width // edge)
+    features = lax.all_gather(x_rows, ("dp", "tensor"), axis=0, tiled=True)
+    partial = pl.pallas_call(
+        forward_kernel,
+        out_shape=jax.ShapeDtypeStruct((tokens, local_width), jnp.bfloat16),
+        in_specs=[SMEM, SMEM, SMEM, VMEM, VMEM],
+        out_specs=VMEM,
+        scratch_shapes=[pltpu.VMEM((tokens, local_width), jnp.float32)],
+        compiler_params=PARAMS,
+        cost_estimate=pl.CostEstimate(
+            flops=2 * cap * tokens * edge * edge,
+            bytes_accessed=2 * tokens * (width + local_width) + 2 * cap * edge * edge,
+            transcendentals=0,
+        ),
+    )(block_row, col_local, block_counts, features, block_weights)
+    pre = lax.psum_scatter(partial, "dp", scatter_dimension=0, tiled=True)
+    act, back = jax.vjp(gelu_tanh, pre.astype(jnp.float32))
+    activation = act.astype(jnp.bfloat16)
+    (pre_grad,) = back(act_grad.astype(jnp.float32))
+    grads_all = lax.all_gather(pre_grad.astype(jnp.bfloat16), "dp", axis=0, tiled=True)
+    grads = pl.pallas_call(
+        gradient_kernel,
+        out_shape=jax.ShapeDtypeStruct(block_weights.shape, jnp.bfloat16),
+        in_specs=[SMEM, SMEM, SMEM, VMEM, VMEM],
+        out_specs=VMEM,
+        compiler_params=PARAMS,
+        cost_estimate=pl.CostEstimate(
+            flops=2 * cap * tokens * edge * edge,
+            bytes_accessed=2 * tokens * (width + local_width) + 2 * cap * edge * edge,
+            transcendentals=0,
+        ),
+    )(block_row, col_local, block_counts, features, grads_all)
+    return (activation, grads)
+
+
+def move_weights(x_rows, block_weights, block_row, block_col, block_counts, act_grad):
     rank = lax.axis_index("tensor")
     n_data = lax.axis_size("dp")
     cap, edge = (block_weights.shape[0], block_weights.shape[1])
@@ -80,6 +168,13 @@
     return (activation, grads)
 
 
+def per_device(x_rows, block_weights, block_row, block_col, block_counts, act_grad):
+    row_bytes = x_rows.size * lax.axis_size("dp") * lax.axis_size("tensor")
+    weight_bytes = block_weights.size * lax.axis_size("dp")
+    plan = move_rows if row_bytes <= weight_bytes else move_weights
+    return plan(x_rows, block_weights, block_row, block_col, block_counts, act_grad)
+
+
 def solution(mesh):
     return jax.shard_map(
         per_device,

time: 917 us -> 260 us (0.28)
  loops' own time: 498 us -> 0 us
  matrix products: 69.3 us -> 0 us
  local copies, waits for them, and re-layouts: 68.4 us -> 2.08 us
  Pallas kernels: 0 us -> 33 us
  blocking collectives: 22.3 us -> 0 us
  waiting for transfers between devices: 226 us -> 206 us
    another operation x1 -> x0, loops' own time: 498 us -> none  [per_device(): pre_three, _ = lax.scan(one_group, pre_three, items)]
    dot_general x50 -> x0, matrix products: 69.3 us -> none  [the longest x49 58.1 us: one_group(): jnp.einsum('rgk,gkm->rgm', selected, w_group, preferred_element_type=jnp....]
    reduce_scatter x1, waiting for transfers between devices: 130 us -> 68.4 us  [move_rows(): pre = lax.psum_scatter(partial, 'dp', scatter_dimension=0, tiled=True)]
    all_gather x1 -> x2, waiting for transfers between devices: 95.1 us -> 137 us  [the longest x1 74 us: move_rows(): features = lax.all_gather(x_rows, ('dp', 'tensor'), axis=0, tiled=True)]
    gather x51 -> x0, local copies, waits for them, and re-layouts: 34 us -> none  [the longest x49 27.6 us: one_group(): selected = jnp.take(features, i_group, axis=1)]
    pallas_call x0 -> x2, Pallas kernels: none -> 33 us  [the longest x1 16.8 us: move_rows(): pl.pallas_call(forward_kernel, out_shape=jax.ShapeDtypeStruct((tokens, lo...]
    slice x49 -> x0, local copies, waits for them, and re-layouts: 32.4 us -> none  [one_group(): target = c_group[member]]
    all_gather x1 -> x0, blocking collectives: 11.7 us -> none  [per_device(): gathered = lax.all_gather(x_rows, 'tensor', axis=0, tiled=True)]
  transfers between devices with their start and end apart: 2 -> 3, of which waited for: 2 -> 3; matrix products, arithmetic and copies ran while one was open for 0% -> 0% of each run, Pallas kernels for 0% -> 0%
where the time goes in v1:
time: 260 us
  waiting for transfers between devices  206 us (79%)
  Pallas kernels  33 us (13%)
  between operations  14.4 us (6%)
  other arithmetic  4.15 us (2%)
    all_gather x1, waiting for transfers between devices, move_rows(): features = lax.all_gather(x_rows, ('dp', 'tensor'), axis=0, tiled=True)  74 us
    reduce_scatter x1, waiting for transfers between devices, move_rows(): pre = lax.psum_scatter(partial, 'dp', scatter_dimension=0, tiled=True)  68.4 us
    all_gather x1, waiting for transfers between devices, move_rows(): lax.all_gather(pre_grad.astype(jnp.bfloat16), 'dp', axis=0, tiled=True)  63.3 us
    pallas_call x1, Pallas kernels, move_rows(): pl.pallas_call(forward_kernel, out_shape=jax.ShapeDtypeStruct((tokens, lo...  16.8 us
    pallas_call x1, Pallas kernels, move_rows(): pl.pallas_call(gradient_kernel, out_shape=jax.ShapeDtypeStruct(block_weig...  16.2 us
  transfers between devices with their start and end apart: 3, of which 3 were waited for; matrix products, arithmetic and copies ran while one was open for 0% of the time, Pallas kernels for 0%

profile of v1, /device:TPU:0, one launch (start us, length us, event | category | flops | bytes accessed | tf_op | source)
XLA Modules:
  0.0 260.1 jit_solution(6314405689619672684)
XLA Ops:
  7.2 0.0 all-gather.3.cloned.1.call-start
  7.2 0.7 all-gather.3.cloned.1.call-update
  7.9 0.0 reduce-scatter.2.cloned.1.call-start
  8.6 0.7 broadcast_subtract_fusion.col_ref
  9.3 74.0 %all-gather.3.cloned.1.call-done.x_ref = bf16[256,12288]{1,0:T(8,128)(2,1)} async-done(((bf16[8,12288]{1,0:T(8,128)(2,1)}), bf16[256,12288]{1,0:T(8,128)(2,1)}) %all-gather.3.cloned.1.call-update) | async-done | bytes 6291472 | tf_op jit(solution)/shard_map/all_gather | solution.py:67
  83.2 0.0 copy-start
  83.2 1.4 copy-done
  84.6 0.0 copy-start.1
  84.6 0.7 copy-done.1
  85.3 16.8 %shard_map.77 = bf16[256,12288]{1,0:T(8,128)(2,1)} custom-call(s32[49]{0:T(128)S(1)} %copy-done.1, s32[49]{0:T(128)S(1)} %broadcast_subtract_fusion.col_ref, s32[1]{0:T(128)S(6)} %copy.8.count_ref, bf16[256,12288]{1,0:T(8,128)(2,1)} %all-gather.3.cloned.1.call-done.x_ref, bf16[49,128,128]{2,1,0:T(8,128)(2,1)S(1)} %copy-done), custom_call_target="tpu_custom_call" | custom-call | flops 411041792 | bytes 14188544 | tf_op jit(solution)/shard_map/pallas_call | solution.py:68
  102.1 0.0 copy-start.3
  102.1 0.0 reduce-scatter.2.cloned.1.call-update
  102.1 0.0 copy-start.2
  102.1 0.0 all-gather.5.cloned.1.call-start
  102.2 68.4 %reduce-scatter.2.cloned.1.call-done = bf16[32,12288]{1,0:T(8,128)(2,1)} async-done(((bf16[256,12288]{1,0:T(8,128)(2,1)}), bf16[32,12288]{1,0:T(8,128)(2,1)}) %reduce-scatter.2.cloned.1.call-update) | async-done | bytes 786448 | tf_op jit(solution)/shard_map/reduce_scatter | solution.py:81
  170.6 0.0 copy-done.3
  170.6 3.5 %fusion.3 = (bf16[32,12288]{1,0:T(8,128)(2,1)}, bf16[32,12288]{1,0:T(8,128)(2,1)}) fusion(bf16[32,12288]{1,0:T(8,128)(2,1)S(1)} %copy-done.3, bf16[32,12288]{1,0:T(8,128)(2,1)} %reduce-scatter.2.cloned.1.call-done), kind=kLoop, calls=%fused_computation.9 | loop fusion | flops 9437184 | bytes 3145728 | tf_op jit(solution)/shard_map/convert_element_type | solution.py:85
  174.1 0.0 all-gather.5.cloned.1.call-update
  174.1 63.3 %all-gather.5.cloned.1.call-done.grad_ref = bf16[256,12288]{1,0:T(8,128)(2,1)} async-done(((bf16[32,12288]{1,0:T(8,128)(2,1)}), bf16[256,12288]{1,0:T(8,128)(2,1)}) %all-gather.5.cloned.1.call-update) | async-done | bytes 6291472 | tf_op jit(solution)/shard_map/all_gather | solution.py:85
  237.4 0.0 copy-done.2
  237.4 16.2 %shard_map.78 = bf16[49,128,128]{2,1,0:T(8,128)(2,1)} custom-call(s32[49]{0:T(128)S(1)} %copy-done.2, s32[49]{0:T(128)S(1)} %broadcast_subtract_fusion.col_ref, s32[1]{0:T(128)S(6)} %copy.8.count_ref, bf16[256,12288]{1,0:T(8,128)(2,1)} %all-gather.3.cloned.1.call-done.x_ref, bf16[256,12288]{1,0:T(8,128)(2,1)} %all-gather.5.cloned.1.call-done.grad_ref), custom_call_target="tpu_custom_call" | custom-call | flops 411041792 | bytes 14188544 | tf_op jit(solution)/shard_map/pallas_call | solution.py:86
Async XLA Ops:
  7.2 76.0 %all-gather.3.cloned.1.call-start = ((), (), s32[]{:S(2)}) async-start(), calls=%async_computation.1 | async-start | bytes 6488064 | tf_op jit(solution)/shard_map/all_gather | solution.py:67
  7.9 162.7 %reduce-scatter.2.cloned.1.call-start = ((), (), s32[]{:S(2)}) async-start(), calls=%async_computation.2 | async-start | bytes 7077888 | tf_op jit(solution)/shard_map/reduce_scatter | solution.py:81
  83.2 1.4 copy-start
  84.6 0.7 copy-start.1
  102.1 68.5 %copy-start.3 = (bf16[32,12288]{1,0:T(8,128)(2,1)S(1)}, bf16[32,12288]{1,0:T(8,128)(2,1)}, u32[]{:S(2)}) copy-start(bf16[32,12288]{1,0:T(8,128)(2,1)} %param.11) | copy-start | bytes 2359300
  102.1 135.3 %copy-start.2 = (s32[49]{0:T(128)S(1)}, s32[49]{0:T(128)}, u32[]{:S(2)}) copy-start(s32[49]{0:T(128)} %row_ref.3) | copy-start | bytes 592
  102.1 135.2 %all-gather.5.cloned.1.call-start = ((), (), s32[]{:S(2)}) async-start(), calls=%async_computation.3 | async-start | bytes 7077888 | tf_op jit(solution)/shard_map/all_gather | solution.py:85
Sparse Core Ops, SparseCore 0:
  10.9 72.2 all-gather.2
  102.2 68.3 reduce-scatter.1
  174.2 63.1 all-gather.4

commit v2 on v1

--- a/solution.py
+++ b/solution.py
@@ -1,4 +1,3 @@
-import functools
 import math
 
 import jax
@@ -13,45 +12,69 @@
     return jax.nn.gelu(value, approximate=True)
 
 
-def forward_kernel(row_ref, col_ref, count_ref, x_ref, w_ref, out_ref, acc_ref):
+def forward_kernel(row_ref, col_ref, count_ref, x_ref, w_ref, *rest):
+    *out_refs, acc_ref = rest
     cap, edge, _ = w_ref.shape
+    group = math.gcd(cap, 7)
     blocks = acc_ref.shape[1] // edge
+    blocks_each = blocks // len(out_refs)
 
     @pl.loop(0, blocks)
     def _(block):
         lanes = pl.ds(pl.multiple_of(block * edge, edge), edge)
         acc_ref[:, lanes] = jnp.zeros((acc_ref.shape[0], edge), jnp.float32)
 
-    @pl.loop(0, count_ref[0])
-    def _(slot):
-        source = pl.ds(pl.multiple_of(row_ref[slot] * edge, edge), edge)
-        target = pl.ds(pl.multiple_of(col_ref[slot] * edge, edge), edge)
-        acc_ref[:, target] += jnp.dot(
-            x_ref[:, source], w_ref[slot], preferred_element_type=jnp.float32
-        )
-
-    @pl.loop(0, blocks)
-    def _(block):
-        lanes = pl.ds(pl.multiple_of(block * edge, edge), edge)
-        out_ref[:, lanes] = acc_ref[:, lanes].astype(out_ref.dtype)
-
-
-def gradient_kernel(row_ref, col_ref, count_ref, x_ref, grad_ref, out_ref):
+    @pl.loop(0, cap // group)
+    def _(step):
+        for member in range(group):
+            slot = step * group + member
+            source = pl.ds(pl.multiple_of(row_ref[slot] * edge, edge), edge)
+            target = pl.ds(pl.multiple_of(col_ref[slot] * edge, edge), edge)
+            product = jnp.dot(
+                x_ref[:, source], w_ref[slot], preferred_element_type=jnp.float32
+            )
+            acc_ref[:, target] += jnp.where(slot < count_ref[0], product, 0.0)
+
+    for part, out_ref in enumerate(out_refs):
+
+        @pl.loop(0, blocks_each)
+        def _(block):
+            place = (block + part * blocks_each) * edge
+            lanes = pl.ds(pl.multiple_of(block * edge, edge), edge)
+            source = pl.ds(pl.multiple_of(place, edge), edge)
+            out_ref[:, lanes] = acc_ref[:, source].astype(out_ref.dtype)
+
+
+def gradient_kernel(row_ref, col_ref, count_ref, x_ref, *rest):
+    *grad_refs, out_ref, all_ref, sems = rest
     cap, edge, _ = out_ref.shape
-
-    @pl.loop(0, cap)
-    def _(slot):
-        source = pl.ds(pl.multiple_of(row_ref[slot] * edge, edge), edge)
-        target = pl.ds(pl.multiple_of(col_ref[slot] * edge, edge), edge)
-        product = lax.dot_general(
-            x_ref[:, source],
-            grad_ref[:, target],
-            (((0,), (0,)), ((), ())),
-            preferred_element_type=jnp.float32,
-        )
-        out_ref[slot] = jnp.where(slot < count_ref[0], product, 0.0).astype(out_ref.dtype)
-
-
+    group = math.gcd(cap, 7)
+    each = all_ref.shape[1] // len(grad_refs)
+    copies = [
+        pltpu.make_async_copy(grad_ref, all_ref.at[:, pl.ds(part * each, each)], sems.at[part])
+        for part, grad_ref in enumerate(grad_refs)
+    ]
+    for copy in copies:
+        copy.start()
+    for copy in copies:
+        copy.wait()
+
+    @pl.loop(0, cap // group)
+    def _(step):
+        for member in range(group):
+            slot = step * group + member
+            source = pl.ds(pl.multiple_of(row_ref[slot] * edge, edge), edge)
+            target = pl.ds(pl.multiple_of(col_ref[slot] * edge, edge), edge)
+            product = lax.dot_general(
+                x_ref[:, source],
+                all_ref[:, target],
+                (((0,), (0,)), ((), ())),
+                preferred_element_type=jnp.float32,
+            )
+            out_ref[slot] = jnp.where(slot < count_ref[0], product, 0.0).astype(out_ref.dtype)
+
+
+PARTS = 2
 SMEM = pl.BlockSpec(memory_space=pltpu.SMEM)
 VMEM = pl.BlockSpec(memory_space=pltpu.VMEM)
 PARAMS = pltpu.CompilerParams(vmem_limit_bytes=48 * 1024 * 1024)
@@ -63,13 +86,14 @@
     width = x_rows.shape[1]
     tokens = x_rows.shape[0] * lax.axis_size("dp") * lax.axis_size("tensor")
     local_width = act_grad.shape[1]
+    each = local_width // PARTS
     col_local = block_col - rank * (local_width // edge)
     features = lax.all_gather(x_rows, ("dp", "tensor"), axis=0, tiled=True)
     partial = pl.pallas_call(
         forward_kernel,
-        out_shape=jax.ShapeDtypeStruct((tokens, local_width), jnp.bfloat16),
+        out_shape=[jax.ShapeDtypeStruct((tokens, each), jnp.bfloat16)] * PARTS,
         in_specs=[SMEM, SMEM, SMEM, VMEM, VMEM],
-        out_specs=VMEM,
+        out_specs=[VMEM] * PARTS,
         scratch_shapes=[pltpu.VMEM((tokens, local_width), jnp.float32)],
         compiler_params=PARAMS,
         cost_estimate=pl.CostEstimate(
@@ -78,23 +102,37 @@
             transcendentals=0,
         ),
     )(block_row, col_local, block_counts, features, block_weights)
-    pre = lax.psum_scatter(partial, "dp", scatter_dimension=0, tiled=True)
-    act, back = jax.vjp(gelu_tanh, pre.astype(jnp.float32))
-    activation = act.astype(jnp.bfloat16)
-    (pre_grad,) = back(act_grad.astype(jnp.float32))
-    grads_all = lax.all_gather(pre_grad.astype(jnp.bfloat16), "dp", axis=0, tiled=True)
+    pre_parts = [
+        lax.psum_scatter(item, "dp", scatter_dimension=0, tiled=True) for item in partial
+    ]
+    activations, grads_all = [], []
+    ready = None
+    for part, pre in enumerate(pre_parts):
+        if ready is not None:
+            _, pre = lax.optimization_barrier((ready, pre))
+        cotangent = act_grad[:, part * each : (part + 1) * each].astype(jnp.float32)
+        act, back = jax.vjp(gelu_tanh, pre.astype(jnp.float32))
+        (pre_grad,) = back(cotangent)
+        activations.append(act.astype(jnp.bfloat16))
+        ready = pre_grad.astype(jnp.bfloat16)
+        grads_all.append(lax.all_gather(ready, "dp", axis=0, tiled=True))
+    activation = jnp.concatenate(activations, axis=1)
     grads = pl.pallas_call(
         gradient_kernel,
         out_shape=jax.ShapeDtypeStruct(block_weights.shape, jnp.bfloat16),
-        in_specs=[SMEM, SMEM, SMEM, VMEM, VMEM],
+        in_specs=[SMEM, SMEM, SMEM, VMEM] + [pl.BlockSpec(memory_space=pl.ANY)] * PARTS,
         out_specs=VMEM,
+        scratch_shapes=[
+            pltpu.VMEM((tokens, local_width), jnp.bfloat16),
+            pltpu.SemaphoreType.DMA((PARTS,)),
+        ],
         compiler_params=PARAMS,
         cost_estimate=pl.CostEstimate(
             flops=2 * cap * tokens * edge * edge,
             bytes_accessed=2 * tokens * (width + local_width) + 2 * cap * edge * edge,
             transcendentals=0,
         ),
-    )(block_row, col_local, block_counts, features, grads_all)
+    )(block_row, col_local, block_counts, features, *grads_all)
     return (activation, grads)
 
 

time: 260 us -> 274 us (1.054)
  waiting for transfers between devices: 206 us -> 228 us
  Pallas kernels: 33 us -> 20.9 us
    all_gather x1 -> x2, waiting for transfers between devices: 63.3 us -> 74.8 us  [move_rows(): grads_all.append(lax.all_gather(ready, 'dp', axis=0, tiled=True))]
    reduce_scatter x1 -> x2, waiting for transfers between devices: 68.4 us -> 77.6 us  [move_rows(): lax.psum_scatter(item, 'dp', scatter_dimension=0, tiled=True)]
    pallas_call x1, Pallas kernels: 16.2 us -> 9.26 us  [move_rows(): pl.pallas_call(gradient_kernel, out_shape=jax.ShapeDtypeStruct(block_weig...]
    pallas_call x1, Pallas kernels: 16.8 us -> 11.6 us  [move_rows(): pl.pallas_call(forward_kernel, out_shape=[jax.ShapeDtypeStruct((tokens, e...]
  transfers between devices with their start and end apart: 3 -> 5, of which waited for: 3 -> 5; matrix products, arithmetic and copies ran while one was open for 0% -> 2% of each run, Pallas kernels for 0% -> 0%
where the time goes in v2:
time: 274 us
  waiting for transfers between devices  228 us (83%)
  Pallas kernels  20.9 us (8%)
  between operations  14.5 us (5%)
  other arithmetic  6.31 us (2%)
  local copies, waits for them, and re-layouts  3.97 us (1%)
    reduce_scatter x2, waiting for transfers between devices, move_rows(): lax.psum_scatter(item, 'dp', scatter_dimension=0, tiled=True)  77.6 us
    all_gather x2, waiting for transfers between devices, move_rows(): grads_all.append(lax.all_gather(ready, 'dp', axis=0, tiled=True))  74.8 us
    all_gather x1, waiting for transfers between devices, move_rows(): features = lax.all_gather(x_rows, ('dp', 'tensor'), axis=0, tiled=True)  74 us
    pallas_call x1, Pallas kernels, move_rows(): pl.pallas_call(forward_kernel, out_shape=[jax.ShapeDtypeStruct((tokens, e...  11.6 us
    pallas_call x1, Pallas kernels, move_rows(): pl.pallas_call(gradient_kernel, out_shape=jax.ShapeDtypeStruct(block_weig...  9.26 us
  transfers between devices with their start and end apart: 5, of which 5 were waited for; matrix products, arithmetic and copies ran while one was open for 2% of the time, Pallas kernels for 0%

profile of v2, /device:TPU:0, one launch (start us, length us, event | category | flops | bytes accessed | tf_op | source)
XLA Modules:
  0.0 273.5 jit_solution(6046000020538648821)
XLA Ops:
  7.2 0.0 all-gather.4.cloned.1.call-start
  7.2 0.7 all-gather.4.cloned.1.call-update
  7.9 0.0 reduce-scatter.3.cloned.1.call-start
  8.6 0.7 broadcast_subtract_fusion.col_ref
  9.3 74.0 %all-gather.4.cloned.1.call-done.x_ref = bf16[256,12288]{1,0:T(8,128)(2,1)} async-done(((bf16[8,12288]{1,0:T(8,128)(2,1)}), bf16[256,12288]{1,0:T(8,128)(2,1)}) %all-gather.4.cloned.1.call-update) | async-done | bytes 6291472 | tf_op jit(solution)/shard_map/all_gather | solution.py:91
  83.2 0.0 copy-start.1
  83.2 1.4 copy-done.1
  84.6 0.0 copy-start.2
  84.6 0.7 copy-done.2
  85.3 11.6 %shard_map.77 = (bf16[256,6144]{1,0:T(8,128)(2,1)}, bf16[256,6144]{1,0:T(8,128)(2,1)}) custom-call(s32[49]{0:T(128)S(1)} %copy-done.2, s32[49]{0:T(128)S(1)} %broadcast_subtract_fusion.col_ref, s32[1]{0:T(128)S(6)} %copy.8.count_ref, bf16[256,12288]{1,0:T(8,128)(2,1)} %all-gather.4.cloned.1.call-done.x_ref, bf16[49,128,128]{2,1,0:T(8,128)(2,1)S(1)} %copy-done.1), custom_call_target="tpu_custom_call" | custom-call | flops 411041792 | bytes 14188544 | tf_op jit(solution)/shard_map/pallas_call | solution.py:92
  96.9 0.0 copy-start.4
  96.9 0.0 reduce-scatter.3.cloned.1.call-update
  96.9 0.0 reduce-scatter.5.cloned.1.call-start
  97.0 0.7 reduce-scatter.5.cloned.1.call-update
  97.6 0.0 copy-start.3
  97.7 0.0 all-gather.6.cloned.1.call-start
  97.7 38.2 %reduce-scatter.3.cloned.1.call-done = bf16[32,6144]{1,0:T(8,128)(2,1)} async-done(((bf16[256,6144]{1,0:T(8,128)(2,1)}), bf16[32,6144]{1,0:T(8,128)(2,1)}) %reduce-scatter.3.cloned.1.call-update) | async-done | bytes 393232 | tf_op jit(solution)/shard_map/reduce_scatter | solution.py:106
  135.9 0.0 copy-done.4
  135.9 2.4 fusion.13
  138.3 0.0 all-gather.6.cloned.1.call-update
  138.3 0.0 all-gather.8.cloned.1.call-start
  138.3 39.3 %reduce-scatter.5.cloned.1.call-done = bf16[32,6144]{1,0:T(8,128)(2,1)} async-done(((bf16[256,6144]{1,0:T(8,128)(2,1)}), bf16[32,6144]{1,0:T(8,128)(2,1)}) %reduce-scatter.5.cloned.1.call-update) | async-done | bytes 393232 | tf_op jit(solution)/shard_map/reduce_scatter | solution.py:106
  177.7 2.4 fusion.7
  180.1 0.0 all-gather.8.cloned.1.call-update
  180.1 0.9 pad_maximum_fusion
  181.0 35.6 %all-gather.6.cloned.1.call-done.rest_0_ = bf16[256,6144]{1,0:T(8,128)(2,1)} async-done(((bf16[32,6144]{1,0:T(8,128)(2,1)}), bf16[256,6144]{1,0:T(8,128)(2,1)}) %all-gather.6.cloned.1.call-update) | async-done | bytes 3145744 | tf_op jit(solution)/shard_map/all_gather | solution.py:118
  216.6 39.2 %all-gather.8.cloned.1.call-done.rest_1_ = bf16[256,6144]{1,0:T(8,128)(2,1)} async-done(((bf16[32,6144]{1,0:T(8,128)(2,1)}), bf16[256,6144]{1,0:T(8,128)(2,1)}) %all-gather.8.cloned.1.call-update) | async-done | bytes 3145744 | tf_op jit(solution)/shard_map/all_gather | solution.py:118
  255.8 0.0 copy-done.3
  255.8 0.0 copy-start
  255.8 1.9 copy-done
  257.7 9.3 %shard_map.78 = bf16[49,128,128]{2,1,0:T(8,128)(2,1)} custom-call(s32[49]{0:T(128)S(1)} %copy-done.3, s32[49]{0:T(128)S(1)} %broadcast_subtract_fusion.col_ref, s32[1]{0:T(128)S(6)} %copy.8.count_ref, bf16[256,12288]{1,0:T(8,128)(2,1)} %all-gather.4.cloned.1.call-done.x_ref, bf16[256,6144]{1,0:T(8,128)(2,1)S(1)} %copy-done, ...), custom_call_target="tpu_custom_call" | custom-call | flops 411041792 | bytes 14188544 | tf_op jit(solution)/shard_map/pallas_call | solution.py:120
Async XLA Ops:
  7.2 76.0 %all-gather.4.cloned.1.call-start = ((), (), s32[]{:S(2)}) async-start(), calls=%async_computation.2 | async-start | bytes 6488064 | tf_op jit(solution)/shard_map/all_gather | solution.py:91
  7.9 128.0 %reduce-scatter.3.cloned.1.call-start = ((), (), s32[]{:S(2)}) async-start(), calls=%async_computation.3 | async-start | bytes 3538944 | tf_op jit(solution)/shard_map/reduce_scatter | solution.py:106
  83.2 1.4 copy-start.1
  84.6 0.7 copy-start.2
  96.9 39.0 %copy-start.4 = (bf16[32,12288]{1,0:T(8,128)(2,1)S(1)}, bf16[32,12288]{1,0:T(8,128)(2,1)}, u32[]{:S(2)}) copy-start(bf16[32,12288]{1,0:T(8,128)(2,1)} %param.11) | copy-start | bytes 2359300
  96.9 80.8 %reduce-scatter.5.cloned.1.call-start = ((), (), s32[]{:S(2)}) async-start(), calls=%async_computation.4 | async-start | bytes 3538944 | tf_op jit(solution)/shard_map/reduce_scatter | solution.py:106
  97.6 158.2 %copy-start.3 = (s32[49]{0:T(128)S(1)}, s32[49]{0:T(128)}, u32[]{:S(2)}) copy-start(s32[49]{0:T(128)} %row_ref.3) | copy-start | bytes 592
  97.7 118.9 %all-gather.6.cloned.1.call-start = ((), (), s32[]{:S(2)}) async-start(), calls=%async_computation.5 | async-start | bytes 3538944 | tf_op jit(solution)/shard_map/all_gather | solution.py:118
  138.3 117.5 %all-gather.8.cloned.1.call-start = ((), (), s32[]{:S(2)}) async-start(), calls=%async_computation.6 | async-start | bytes 3538944 | tf_op jit(solution)/shard_map/all_gather | solution.py:118
  255.8 1.9 copy-start
Sparse Core Ops, SparseCore 0:
  10.9 72.2 all-gather.3
  97.0 38.8 reduce-scatter.2
  138.2 39.4 reduce-scatter.4
  179.2 37.3 all-gather.5
  218.6 37.1 all-gather.7
